TPU v7x, 32 devices: a whole 2x2x4 slice. The times are simulated.
32 devices in a mesh: dp: 4 (over z), bank: 4 (over y, x), head: 2 (over core).
Axes of the slice: x: 2, y: 2, z: 4, core: 2. Of those that a mesh axis runs over, the one named last changes fastest.
Arguments:
- feats: bfloat16 [2048, 2048], P('dp'), may hold values from -6 to 6
- w_first: bfloat16 [2048, 2048], P(None, ('bank', 'head')), may hold values from -0.125 to 0.125
- w_second: bfloat16 [2048, 256], P(('bank', 'head')), may hold values from -0.125 to 0.125
- fresh_keys: float32 [2048, 256], P('dp'), may hold values from -6 to 6
- bank: float32 [32768, 256], P(('bank', 'head'))
- block_lists: int32 [4, 32], P('dp'), may hold values from 0 to 63, as said below
- dest_rows: int32 [2048], P('dp'), may hold values from 0 to 32767, as said below
Outputs:
- loss: float32 [2048], P('dp')
- grad_first: float32 [2048, 2048], P('dp', ('bank', 'head'))
- grad_second: float32 [2048, 256], P(('bank', 'head'))
- new_bank: float32 [32768, 256], P(('bank', 'head'))
Inputs may be any that keep to these rules, and one draw needn't show every extreme that they name: `block_lists`: each row names 32 different blocks. `dest_rows`: all entries differ; the 512 entries of query block g name exactly 64 rows in each range of rows o * 4096 to (o + 1) * 4096 - 1.
All inputs are finite; a program needn't handle non-finite values.
Results may differ from a plain program's by a relative error of at most 0.012.
Values sent between devices are 32-bit elements; how exact they have to be, the bound alone decides.
A program may use at most 128 MiB of HBM per device.

v0:
```python
import jax
import jax.numpy as jnp
from jax import lax
from jax.sharding import PartitionSpec as P

BLOCK = 512
sharpness_divisor = 0.2
epsilon = 1e-06
lowest = -1e30


def joined(array, axis, combine):
    everything = jax.tree.map(lambda part: lax.all_gather(part, axis), array)
    leading = jax.tree.map(lambda part: part[0], everything)

    def hop(k, so_far):
        return combine(so_far, jax.tree.map(lambda part: part[k], everything))

    return lax.fori_loop(1, lax.axis_size(axis), hop, leading)


def unit_rows(values):
    norms = jnp.sqrt(jnp.sum(values * values, axis=1, keepdims=True) + epsilon)
    return (values / norms, norms)


def exact_scores(anchor_matrix, bank_entries):
    return (
        lax.dot_general(
            anchor_matrix,
            bank_entries,
            (((1,), (1,)), ((), ())),
            precision=lax.Precision.HIGHEST,
            preferred_element_type=jnp.float32,
        )
        / sharpness_divisor
    )


def join_stats(first, second):
    best = jnp.maximum(first[0], second[0])
    partition_total = first[1] * jnp.exp(first[0] - best) + second[1] * jnp.exp(second[0] - best)
    return (best, partition_total)


def shards(feats, w_first, w_second, fresh_keys, bank, block_lists, dest_rows):
    owner = lax.axis_index(("bank", "head"))
    owner_rows = bank.shape[0]
    hidden = jnp.maximum(jnp.dot(feats, w_first, preferred_element_type=jnp.float32), 0.0).astype(
        jnp.bfloat16
    )
    partial_embed = jnp.dot(hidden, w_second, preferred_element_type=jnp.float32)
    embed = lax.psum(partial_embed, ("bank", "head"))
    anchor_matrix, norms = unit_rows(embed)
    unit_length_bank, unused = unit_rows(fresh_keys)
    matching_similarity = jnp.sum(anchor_matrix * unit_length_bank, axis=1) / sharpness_divisor
    listed = block_lists[0]
    blocks_here = owner_rows // BLOCK
    owned = listed // blocks_here == owner
    owned_count = jnp.sum(owned.astype(jnp.int32))
    order = jnp.argsort(jnp.where(owned, 0, 1).astype(jnp.int32), stable=True)
    local_blocks = listed[order] - owner * blocks_here
    row_count = anchor_matrix.shape[0]

    def block_keys(index):
        return lax.dynamic_slice_in_dim(bank, local_blocks[index] * BLOCK, BLOCK, 0)

    start_best = jnp.full((row_count,), lowest, jnp.float32)
    start_total = jnp.zeros((row_count,), jnp.float32)
    start_weighted = jnp.zeros((row_count, anchor_matrix.shape[1]), jnp.float32)

    def first_pass(index, carry):
        best, partition_total = carry
        similarity_matrix = exact_scores(anchor_matrix, block_keys(index))
        new_best = jnp.maximum(best, jnp.max(similarity_matrix, axis=1))
        partition_total = partition_total * jnp.exp(best - new_best) + jnp.sum(
            jnp.exp(similarity_matrix - new_best[:, None]), axis=1
        )
        return (new_best, partition_total)

    local_stats = lax.fori_loop(0, owned_count, first_pass, (start_best, start_total))
    neg_best, neg_total = joined(local_stats, ("bank", "head"), join_stats)
    best = jnp.maximum(neg_best, matching_similarity)
    positive_weight = jnp.exp(matching_similarity - best)
    partition_total = neg_total * jnp.exp(neg_best - best) + positive_weight

    def second_pass(index, probability_mixed_bank):
        bank_entries = block_keys(index)
        shares = (
            jnp.exp(exact_scores(anchor_matrix, bank_entries) - best[:, None])
            / partition_total[:, None]
        )
        return probability_mixed_bank + jnp.dot(
            shares,
            bank_entries,
            precision=lax.Precision.HIGHEST,
            preferred_element_type=jnp.float32,
        )

    local_weighted = lax.fori_loop(0, owned_count, second_pass, start_weighted)
    probability_mixed_bank = lax.psum(local_weighted, ("bank", "head"))
    loss = best + jnp.log(partition_total) - matching_similarity
    anchor_derivative = (
        probability_mixed_bank
        + (positive_weight / partition_total - 1.0)[:, None] * unit_length_bank
    ) / sharpness_divisor
    inner = jnp.sum(anchor_matrix * anchor_derivative, axis=1, keepdims=True)
    grad_z = ((anchor_derivative - anchor_matrix * inner) / norms).astype(jnp.bfloat16)
    second_part = lax.dot_general(
        hidden, grad_z, (((0,), (0,)), ((), ())), preferred_element_type=jnp.float32
    )
    grad_second = lax.psum(second_part, "dp")
    grad_hidden = lax.dot_general(
        grad_z, w_second, (((1,), (1,)), ((), ())), preferred_element_type=jnp.float32
    )
    grad_pre = jnp.where(hidden > 0, grad_hidden, 0.0).astype(jnp.bfloat16)
    grad_first = lax.psum_scatter(
        lax.dot_general(
            feats, grad_pre, (((0,), (0,)), ((), ())), preferred_element_type=jnp.float32
        ),
        "dp",
        scatter_dimension=0,
        tiled=True,
    )
    got_keys, got_dest = (
        lax.all_gather(unit_length_bank, "dp", axis=0, tiled=True),
        lax.all_gather(dest_rows.astype(jnp.float32), "dp", axis=0, tiled=True),
    )
    local_rows = got_dest.astype(jnp.int32) - owner * owner_rows
    inside = (local_rows >= 0) & (local_rows < owner_rows)
    new_bank = bank.at[jnp.where(inside, local_rows, owner_rows)].set(got_keys, mode="drop")
    return (loss, grad_first, grad_second, new_bank)


def solution(mesh):
    return jax.shard_map(
        shards,
        mesh=mesh,
        in_specs=(
            P("dp", None),
            P(None, ("bank", "head")),
            P(("bank", "head"), None),
            P("dp", None),
            P(("bank", "head"), None),
            P("dp", None),
            P("dp"),
        ),
        out_specs=(
            P("dp"),
            P("dp", ("bank", "head")),
            P(("bank", "head"), None),
            P(("bank", "head"), None),
        ),
        check_vma=False,
    )
```

profile of v0, /device:TPU:0, one launch (start us, length us, event | category | flops | bytes accessed | tf_op | source)
XLA Modules:
  0.0 383.6 jit_solution(11246029741084995186)
XLA Ops:
  7.2 4.6 %copy.49 = f32[4096,256]{1,0:T(8,128)} copy(f32[4096,256]{1,0:T(8,128)} %param.17) | data formatting | bytes 8388608
  17.1 54.1 %all-reduce.4.cloned.1.call-done = f32[512,256]{1,0:T(8,128)} async-done(((f32[512,256]{1,0:T(8,128)}), f32[512,256]{1,0:T(8,128)}) %all-reduce.4.cloned.1.call-update) | async-done | bytes 524304 | tf_op jit(solution)/shard_map/psum | solution.py:53
  74.5 36.0 %while.39 = (s32[]{:T(128)}, f32[512]{0:T(512)S(1)}, f32[512]{0:T(512)S(1)}, s32[]{:T(128)}, s32[32]{0:T(128)S(1)}, /*index=5*/f32[4096,256]{1,0:T(8,128)}, f32[...) while((s32[]{:T(128)}, f32[512]{0:T(512)S(1)}, ...), condition=%wide.region_7.8_spmd, body=%wide.region_4.0_spmd.sunk | while | flops 806355968 | bytes 3172573 | solution.py:81
  110.5 7.4 %all-gather.2 = f32[8,1,512]{2,1,0:T(1,128)S(1)} all-gather(f32[1,1,512]{2,1,0:T(1,128)S(1)} %bitcast.49), channel_id=2, replica_groups=mesh['dp'=4,'bank'=4,'head'=2] {'bank','head'}, dimensions={0}, use_global_device_ids=true | all-gather | bytes 18432 | tf_op jit(solution)/shard_map/all_gather | solution.py:13
  118.0 9.4 %all-gather.3 = f32[8,1,512]{2,1,0:T(1,128)S(1)} all-gather(f32[1,1,512]{2,1,0:T(1,128)S(1)} %bitcast.52), channel_id=3, replica_groups=mesh['dp'=4,'bank'=4,'head'=2] {'bank','head'}, dimensions={0}, use_global_device_ids=true | all-gather | bytes 18432 | tf_op jit(solution)/shard_map/all_gather | solution.py:13
  128.4 62.4 %while.41 = (s32[]{:T(128)}, f32[512,256]{1,0:T(8,128)S(1)}, s32[]{:T(128)}, s32[32]{0:T(128)}, f32[4096,256]{1,0:T(8,128)}, /*index=5*/f32[512,256]{1,0:T(8,128...) while((s32[]{:T(128)}, f32[512,256]{1,0:T(8,128)S(1)}, ...), condition=%wide.region_13.14_spmd, body=%wide.region_12.13_spmd.sunk | while | flops 1611530240 | bytes 4722921 | solution.py:100
  130.9 2.2 fusion.45
  133.1 3.0 convolution_add_fusion.2
  140.8 3.0 convolution_add_fusion.2
  148.5 3.0 convolution_add_fusion.2
  154.1 2.2 fusion.45
  156.3 3.0 convolution_add_fusion.2
  164.0 3.0 convolution_add_fusion.2
  169.5 2.2 fusion.45
  171.7 3.0 convolution_add_fusion.2
  179.4 3.0 convolution_add_fusion.2
  187.1 3.0 convolution_add_fusion.2
  192.4 52.9 %all-reduce.6.cloned.1.call-done = f32[512,256]{1,0:T(8,128)} async-done(((f32[512,256]{1,0:T(8,128)}), f32[512,256]{1,0:T(8,128)}) %all-reduce.6.cloned.1.call-update) | async-done | bytes 524304 | tf_op jit(solution)/shard_map/psum | solution.py:101
  248.8 3.3 convolution_bitcast_fusion
  252.8 12.1 %all-gather.4 = f32[4,1,512]{2,1,0:T(1,128)S(1)} all-gather(f32[1,1,512]{2,1,0:T(1,128)S(1)} %bitcast.58), channel_id=1, replica_groups=mesh['dp'=4,'bank'=4,'head'=2] {'dp'}, dimensions={0}, use_global_device_ids=true | all-gather | bytes 10240 | tf_op jit(solution)/shard_map/all_gather | solution.py:127
  265.9 27.0 %all-gather.7.cloned.1.call-done = f32[2048,256]{1,0:T(8,128)} async-done(((f32[512,256]{1,0:T(8,128)}), f32[2048,256]{1,0:T(8,128)}) %all-gather.7.cloned.1.call-update) | async-done | bytes 2097168 | tf_op jit(solution)/shard_map/all_gather | solution.py:126
  292.9 13.6 %scatter_fusion = f32[4096,256]{1,0:T(8,128)} fusion(f32[4096,256]{1,0:T(8,128)} %get-tuple-element.541, s32[2048]{0:T(1024)S(1)} %compare_select_fusion, f32[2048,256]{1,0:T(8,128)} %all-gather.7.cloned.1.call-done), kind=kCustom, calls=%fused_computation.1 | custom fusion | bytes 6299648 | tf_op jit(solution)/shard_map/scatter | solution.py:131
  306.5 31.3 %reduce-scatter.2.cloned.1.call-done = f32[512,256]{0,1:T(8,128)} async-done(((f32[2048,256]{0,1:T(8,128)}), f32[512,256]{0,1:T(8,128)}) %reduce-scatter.2.cloned.1.call-update) | async-done | bytes 524304 | tf_op jit(solution)/shard_map/reduce_scatter | solution.py:117
  339.9 35.6 %all-reduce.8.cloned.1.call-done = f32[256,256]{1,0:T(8,128)} async-done(((f32[256,256]{1,0:T(8,128)}), f32[256,256]{1,0:T(8,128)}) %all-reduce.8.cloned.1.call-update) | async-done | bytes 262160 | tf_op jit(solution)/shard_map/psum | solution.py:112
  (136 shorter events, 65.0 us)
Async XLA Ops:
  7.2 4.7 %copy-start = (bf16[512,2048]{1,0:T(8,128)(2,1)S(1)}, bf16[512,2048]{1,0:T(8,128)(2,1)}, u32[]{:S(2)}) copy-start(bf16[512,2048]{1,0:T(8,128)(2,1)} %param.13) | copy-start | bytes 6291460
  7.2 64.1 %all-reduce.4.cloned.1.call-start = ((), (), s32[]{:S(2)}) async-start(), calls=%async_computation.1 | async-start | bytes 1048576 | tf_op jit(solution)/shard_map/psum | solution.py:53
  7.2 4.6 %copy-start.9 = (bf16[2048,256]{1,0:T(8,128)(2,1)S(1)}, bf16[2048,256]{1,0:T(8,128)(2,1)}, u32[]{:S(2)}) copy-start(bf16[2048,256]{1,0:T(8,128)(2,1)} %param.14) | copy-start | bytes 3145732
  11.9 0.9 copy-start.6
  11.9 2.0 copy-start.1
  11.9 5.1 %copy-start.5 = (f32[512,256]{1,0:T(8,128)S(1)}, f32[512,256]{1,0:T(8,128)}, u32[]{:S(2)}) copy-start(f32[512,256]{1,0:T(8,128)} %param.16) | copy-start | bytes 1572868
  13.8 231.5 %all-reduce.6.cloned.1.call-start = ((), (), s32[]{:S(2)}) async-start(), calls=%async_computation.2 | async-start | bytes 1048576 | tf_op jit(solution)/shard_map/psum | solution.py:101
  110.5 17.2 %copy-start.8 = (s32[32]{0:T(128)}, s32[32]{0:T(128)S(1)}, u32[]{:S(2)}) copy-start(s32[32]{0:T(128)S(1)} %get-tuple-element.559) | copy-start | bytes 388
  190.8 0.8 copy-start.2
  191.6 55.2 %copy-start.3 = (f32[512,256]{1,0:T(8,128)S(1)}, f32[512,256]{1,0:T(8,128)}, u32[]{:S(2)}) copy-start(f32[512,256]{1,0:T(8,128)} %get-tuple-element.283) | copy-start | bytes 1572868
  191.6 101.3 %all-gather.7.cloned.1.call-start = ((), (), s32[]{:S(2)}) async-start(), calls=%async_computation.5 | async-start | bytes 2621440 | tf_op jit(solution)/shard_map/all_gather | solution.py:126
  192.4 145.5 %reduce-scatter.2.cloned.1.call-start = ((), (), s32[]{:S(2)}) async-start(), calls=%async_computation.3 | async-start | bytes 2621440 | tf_op jit(solution)/shard_map/reduce_scatter | solution.py:117
  252.1 0.7 copy-start.7
  252.1 12.8 %copy-start.4 = (bf16[512,256]{1,0:T(8,128)(2,1)S(1)}, bf16[512,256]{1,0:T(8,128)(2,1)}, u32[]{:S(2)}) copy-start(bf16[512,256]{1,0:T(8,128)(2,1)} %divide_convert_fusion) | copy-start | bytes 786436
  252.2 123.3 %all-reduce.8.cloned.1.call-start = ((), (), s32[]{:S(2)}) async-start(), calls=%async_computation.4 | async-start | bytes 524288 | tf_op jit(solution)/shard_map/psum | solution.py:112
Sparse Core Ops, SparseCore 0:
  13.9 57.2 all-reduce.3
  191.8 53.5 all-reduce.5
  247.5 45.3 all-gather.6
  295.1 42.7 reduce-scatter.1
  340.7 34.6 all-reduce.7
where the time goes:
time: 386 us; the launch traced here: 384 us
  waiting for transfers between devices  202 us (52%)
  matrix products  64.2 us (17%)
  local copies, waits for them, and re-layouts  39.8 us (10%)
  blocking collectives  28.9 us (7%)
  loops' own time  23.3 us (6%)
  between operations  14 us (4%)
  other arithmetic  11.7 us (3%)
    psum x1, waiting for transfers between devices, shards(): embed = lax.psum(partial_embed, ('bank', 'head'))  54.1 us
    psum x1, waiting for transfers between devices, shards(): probability_mixed_bank = lax.psum(local_weighted, ('bank', 'head'))  52.9 us
    psum x1, waiting for transfers between devices, shards(): grad_second = lax.psum(second_part, 'dp')  35.6 us
    dot_general x16, matrix products, exact_scores(): lax.dot_general(anchor_matrix, bank_entries, (((1,), (1,)), ((), ())), pr...  34.4 us
    reduce_scatter x1, waiting for transfers between devices, shards(): lax.psum_scatter(lax.dot_general(feats, grad_pre, (((0,), (0,)), ((), ())...  31.3 us
    all_gather x1, waiting for transfers between devices, shards(): lax.all_gather(unit_length_bank, 'dp', axis=0, tiled=True)  27 us
    dot_general x8, matrix products, second_pass(): jnp.dot(shares, bank_entries, precision=lax.Precision.HIGHEST, preferred_...  23.8 us
    all_gather x2, blocking collectives, joined(): everything = jax.tree.map(lambda part: lax.all_gather(part, axis), array)  16.8 us
  transfers between devices with their start and end apart: 5, of which 5 were waited for; matrix products, arithmetic and copies ran while one was open for 7% of the time, Pallas kernels for 0%

commit v1 on v0

--- a/solution.py
+++ b/solution.py
@@ -50,7 +50,7 @@
         jnp.bfloat16
     )
     partial_embed = jnp.dot(hidden, w_second, preferred_element_type=jnp.float32)
-    embed = lax.psum(partial_embed, ("bank", "head"))
+    embed = lax.psum(lax.psum(partial_embed, "head"), "bank")
     anchor_matrix, norms = unit_rows(embed)
     unit_length_bank, unused = unit_rows(fresh_keys)
     matching_similarity = jnp.sum(anchor_matrix * unit_length_bank, axis=1) / sharpness_divisor

time: 386 us -> 400 us (1.036)
  waiting for transfers between devices: 202 us -> 215 us
    psum x1 -> x2, waiting for transfers between devices: 54.1 us -> 68 us  [shards(): embed = lax.psum(lax.psum(partial_embed, 'head'), 'bank')]
  transfers between devices with their start and end apart: 5 -> 6, of which waited for: 5 -> 6; matrix products, arithmetic and copies ran while one was open for 7% -> 7% of each run, Pallas kernels for 0% -> 0%
where the time goes in v1:
time: 400 us; the launch traced here: 398 us
  waiting for transfers between devices  215 us (54%)
  matrix products  64.1 us (16%)
  local copies, waits for them, and re-layouts  39.8 us (10%)
  blocking collectives  28.8 us (7%)
  loops' own time  23.3 us (6%)
  between operations  14.3 us (4%)
  other arithmetic  11.8 us (3%)
    psum x2, waiting for transfers between devices, shards(): embed = lax.psum(lax.psum(partial_embed, 'head'), 'bank')  68 us
    psum x1, waiting for transfers between devices, shards(): probability_mixed_bank = lax.psum(local_weighted, ('bank', 'head'))  53.2 us
    psum x1, waiting for transfers between devices, shards(): grad_second = lax.psum(second_part, 'dp')  35.5 us
    dot_general x16, matrix products, exact_scores(): lax.dot_general(anchor_matrix, bank_entries, (((1,), (1,)), ((), ())), pr...  34.3 us
    reduce_scatter x1, waiting for transfers between devices, shards(): lax.psum_scatter(lax.dot_general(feats, grad_pre, (((0,), (0,)), ((), ())...  31.2 us
    all_gather x1, waiting for transfers between devices, shards(): lax.all_gather(unit_length_bank, 'dp', axis=0, tiled=True)  26.8 us
    dot_general x8, matrix products, second_pass(): jnp.dot(shares, bank_entries, precision=lax.Precision.HIGHEST, preferred_...  23.8 us
    all_gather x2, blocking collectives, joined(): everything = jax.tree.map(lambda part: lax.all_gather(part, axis), array)  16.8 us
  transfers between devices with their start and end apart: 6, of which 6 were waited for; matrix products, arithmetic and copies ran while one was open for 7% of the time, Pallas kernels for 0%

profile of v1, /device:TPU:0, one launch (start us, length us, event | category | flops | bytes accessed | tf_op | source)
XLA Modules:
  0.0 397.8 jit_solution(18245808857279872914)
XLA Ops:
  7.2 4.6 %copy.50 = f32[4096,256]{1,0:T(8,128)} copy(f32[4096,256]{1,0:T(8,128)} %param.17) | data formatting | bytes 8388608
  16.3 19.1 %all-reduce.5.cloned.1.call-done = f32[512,256]{1,0:T(8,128)} async-done(((f32[512,256]{1,0:T(8,128)}), f32[512,256]{1,0:T(8,128)}) %all-reduce.5.cloned.1.call-update) | async-done | bytes 524304 | tf_op jit(solution)/shard_map/psum | solution.py:53
  36.4 48.9 %all-reduce.7.cloned.1.call-done = f32[512,256]{1,0:T(8,128)} async-done(((f32[512,256]{1,0:T(8,128)}), f32[512,256]{1,0:T(8,128)}) %all-reduce.7.cloned.1.call-update) | async-done | bytes 524304 | tf_op jit(solution)/shard_map/psum | solution.py:53
  88.5 36.0 %while.39 = (s32[]{:T(128)}, f32[512]{0:T(512)S(1)}, f32[512]{0:T(512)S(1)}, s32[]{:T(128)}, s32[32]{0:T(128)S(1)}, /*index=5*/f32[4096,256]{1,0:T(8,128)}, f32[...) while((s32[]{:T(128)}, f32[512]{0:T(512)S(1)}, ...), condition=%wide.region_8.9_spmd, body=%wide.region_5.0_spmd.sunk | while | flops 806355968 | bytes 3172573 | solution.py:81
  124.6 7.4 %all-gather.2 = f32[8,1,512]{2,1,0:T(1,128)S(1)} all-gather(f32[1,1,512]{2,1,0:T(1,128)S(1)} %bitcast.49), channel_id=2, replica_groups=mesh['dp'=4,'bank'=4,'head'=2] {'bank','head'}, dimensions={0}, use_global_device_ids=true | all-gather | bytes 18432 | tf_op jit(solution)/shard_map/all_gather | solution.py:13
  132.0 9.4 %all-gather.3 = f32[8,1,512]{2,1,0:T(1,128)S(1)} all-gather(f32[1,1,512]{2,1,0:T(1,128)S(1)} %bitcast.52), channel_id=3, replica_groups=mesh['dp'=4,'bank'=4,'head'=2] {'bank','head'}, dimensions={0}, use_global_device_ids=true | all-gather | bytes 18432 | tf_op jit(solution)/shard_map/all_gather | solution.py:13
  142.4 62.4 %while.41 = (s32[]{:T(128)}, f32[512,256]{1,0:T(8,128)S(1)}, s32[]{:T(128)}, s32[32]{0:T(128)}, f32[4096,256]{1,0:T(8,128)}, /*index=5*/f32[512,256]{1,0:T(8,128...) while((s32[]{:T(128)}, f32[512,256]{1,0:T(8,128)S(1)}, ...), condition=%wide.region_14.15_spmd, body=%wide.region_13.14_spmd.sunk | while | flops 1611530240 | bytes 4722921 | solution.py:100
  144.9 2.2 fusion.45
  147.1 3.0 convolution_add_fusion.2
  154.8 3.0 convolution_add_fusion.2
  162.6 3.0 convolution_add_fusion.2
  168.1 2.2 fusion.45
  170.3 3.0 convolution_add_fusion.2
  178.0 3.0 convolution_add_fusion.2
  185.7 3.0 convolution_add_fusion.2
  193.4 3.0 convolution_add_fusion.2
  201.1 3.0 convolution_add_fusion.2
  206.3 53.2 %all-reduce.9.cloned.1.call-done = f32[512,256]{1,0:T(8,128)} async-done(((f32[512,256]{1,0:T(8,128)}), f32[512,256]{1,0:T(8,128)}) %all-reduce.9.cloned.1.call-update) | async-done | bytes 524304 | tf_op jit(solution)/shard_map/psum | solution.py:101
  262.9 3.3 convolution_bitcast_fusion
  266.9 12.1 %all-gather.4 = f32[4,1,512]{2,1,0:T(1,128)S(1)} all-gather(f32[1,1,512]{2,1,0:T(1,128)S(1)} %bitcast.58), channel_id=1, replica_groups=mesh['dp'=4,'bank'=4,'head'=2] {'dp'}, dimensions={0}, use_global_device_ids=true | all-gather | bytes 10240 | tf_op jit(solution)/shard_map/all_gather | solution.py:127
  280.0 26.8 %all-gather.7.cloned.1.call-done = f32[2048,256]{1,0:T(8,128)} async-done(((f32[512,256]{1,0:T(8,128)}), f32[2048,256]{1,0:T(8,128)}) %all-gather.7.cloned.1.call-update) | async-done | bytes 2097168 | tf_op jit(solution)/shard_map/all_gather | solution.py:126
  306.9 13.6 %scatter_fusion = f32[4096,256]{1,0:T(8,128)} fusion(f32[4096,256]{1,0:T(8,128)} %get-tuple-element.542, s32[2048]{0:T(1024)S(1)} %compare_select_fusion, f32[2048,256]{1,0:T(8,128)} %all-gather.7.cloned.1.call-done), kind=kCustom, calls=%fused_computation.1 | custom fusion | bytes 6299648 | tf_op jit(solution)/shard_map/scatter | solution.py:131
  320.5 31.2 %reduce-scatter.2.cloned.1.call-done = f32[512,256]{0,1:T(8,128)} async-done(((f32[2048,256]{0,1:T(8,128)}), f32[512,256]{0,1:T(8,128)}) %reduce-scatter.2.cloned.1.call-update) | async-done | bytes 524304 | tf_op jit(solution)/shard_map/reduce_scatter | solution.py:117
  353.7 35.5 %all-reduce.11.cloned.1.call-done = f32[256,256]{1,0:T(8,128)} async-done(((f32[256,256]{1,0:T(8,128)}), f32[256,256]{1,0:T(8,128)}) %all-reduce.11.cloned.1.call-update) | async-done | bytes 262160 | tf_op jit(solution)/shard_map/psum | solution.py:112
  (139 shorter events, 67.2 us)
Async XLA Ops:
  7.2 4.7 %copy-start = (bf16[512,2048]{1,0:T(8,128)(2,1)S(1)}, bf16[512,2048]{1,0:T(8,128)(2,1)}, u32[]{:S(2)}) copy-start(bf16[512,2048]{1,0:T(8,128)(2,1)} %param.13) | copy-start | bytes 6291460
  7.2 28.3 %all-reduce.5.cloned.1.call-start = ((), (), s32[]{:S(2)}) async-start(), calls=%async_computation.1 | async-start | bytes 1048576 | tf_op jit(solution)/shard_map/psum | solution.py:53
  7.2 4.6 %copy-start.9 = (bf16[2048,256]{1,0:T(8,128)(2,1)S(1)}, bf16[2048,256]{1,0:T(8,128)(2,1)}, u32[]{:S(2)}) copy-start(bf16[2048,256]{1,0:T(8,128)(2,1)} %param.14) | copy-start | bytes 3145732
  11.9 0.9 copy-start.6
  11.9 2.0 copy-start.1
  12.8 22.7 %copy-start.5 = (f32[512,256]{1,0:T(8,128)S(1)}, f32[512,256]{1,0:T(8,128)}, u32[]{:S(2)}) copy-start(f32[512,256]{1,0:T(8,128)} %param.16) | copy-start | bytes 1572868
  13.8 71.4 %all-reduce.7.cloned.1.call-start = ((), (), s32[]{:S(2)}) async-start(), calls=%async_computation.2 | async-start | bytes 1048576 | tf_op jit(solution)/shard_map/psum | solution.py:53
  35.5 224.0 %all-reduce.9.cloned.1.call-start = ((), (), s32[]{:S(2)}) async-start(), calls=%async_computation.3 | async-start | bytes 1048576 | tf_op jit(solution)/shard_map/psum | solution.py:101
  124.5 17.2 %copy-start.8 = (s32[32]{0:T(128)}, s32[32]{0:T(128)S(1)}, u32[]{:S(2)}) copy-start(s32[32]{0:T(128)S(1)} %get-tuple-element.563) | copy-start | bytes 388
  204.8 0.8 copy-start.2
  205.7 55.2 %copy-start.3 = (f32[512,256]{1,0:T(8,128)S(1)}, f32[512,256]{1,0:T(8,128)}, u32[]{:S(2)}) copy-start(f32[512,256]{1,0:T(8,128)} %get-tuple-element.283) | copy-start | bytes 1572868
  205.7 101.2 %all-gather.7.cloned.1.call-start = ((), (), s32[]{:S(2)}) async-start(), calls=%async_computation.6 | async-start | bytes 2621440 | tf_op jit(solution)/shard_map/all_gather | solution.py:126
  206.2 145.4 %reduce-scatter.2.cloned.1.call-start = ((), (), s32[]{:S(2)}) async-start(), calls=%async_computation.4 | async-start | bytes 2621440 | tf_op jit(solution)/shard_map/reduce_scatter | solution.py:117
  266.2 0.7 copy-start.7
  266.2 12.7 %copy-start.4 = (bf16[512,256]{1,0:T(8,128)(2,1)S(1)}, bf16[512,256]{1,0:T(8,128)(2,1)}, u32[]{:S(2)}) copy-start(bf16[512,256]{1,0:T(8,128)(2,1)} %divide_convert_fusion) | copy-start | bytes 786436
  266.3 123.0 %all-reduce.11.cloned.1.call-start = ((), (), s32[]{:S(2)}) async-start(), calls=%async_computation.5 | async-start | bytes 524288 | tf_op jit(solution)/shard_map/psum | solution.py:112
Sparse Core Ops, SparseCore 0:
  13.9 21.4 all-reduce.4
  38.7 46.5 all-reduce.6
  205.8 53.6 all-reduce.8
  261.5 45.3 all-gather.6
  309.0 42.6 reduce-scatter.1
  354.6 34.6 all-reduce.10
